TPU v7x, 32 devices: a whole 2x2x4 slice. The times are simulated.
32 devices in a mesh: row: 4 (over x, core), col: 8 (over z, y).
Axes of the slice: x: 2, y: 2, z: 4, core: 2. Of those that a mesh axis runs over, the one named last changes fastest.
Arguments:
- contact: bfloat16 [256, 16384], P('row', 'col'), may hold values from -6 to 6
- first_down: bfloat16 [2, 3, 3, 32, 64], replicated, may hold values from -0.25 to 0.25
- first_down_bias: float32 [2, 32], replicated, may hold values from -1.5 to 1.5
- first_up: bfloat16 [2, 3, 3, 64, 32], replicated, may hold values from -0.375 to 0.375
- first_up_bias: float32 [2, 64], replicated, may hold values from -1.5 to 1.5
- second_down: bfloat16 [2, 3, 3, 32, 64], replicated, may hold values from -0.25 to 0.25
- second_down_bias: float32 [2, 32], replicated, may hold values from -1.5 to 1.5
- second_up: bfloat16 [2, 3, 3, 64, 32], replicated, may hold values from -0.375 to 0.375
- second_up_bias: float32 [2, 64], replicated, may hold values from -1.5 to 1.5
Outputs:
- decoded: bfloat16 [256, 16384], P('row', 'col')
All inputs are finite; a program needn't handle non-finite values.
Results may differ from a plain program's by a relative error of at most 0.012.
Values may be sent and summed in bfloat16 or wider, within the bound.
A program may use at most 64 MiB of HBM per device.

v0:
```python
import functools

import jax
import jax.numpy as jnp
from jax import lax
from jax.experimental import pallas as pl
from jax.experimental.pallas import tpu as pltpu
from jax.sharding import PartitionSpec as P

MESH = pl.DeviceIdType.MESH
HALO = 16
SIDE = HALO // 2
BLOCKS = ((1, 2), (4, 8))
SIDES = ((0, -1), (0, 1))
ENDS = ((-1, 0), (1, 0))
CORNERS = ((-1, -1), (-1, 1), (1, -1), (1, 1))


def chunk_of(count, most):
    return max(n for n in range(1, most + 1) if count % n == 0)


def kernel(
    rows_of, cols_of,
    contact, *refs,
):
    weights, (out,), held = refs[:8], refs[8:9], refs[9:17]
    (
    v1, v2, middle, hid1, hid2, first, mirror, passing, wide, flipped, wide_down, wd, wu, bias,
    send1, recv1, send2, recv2, send_m, recv_m, pass_recv, pass_send, local_sem, load_sem, weight_sem,
    ) = refs[17:]
    fd, fdb, fu, fub, sd, sdb, su, sub = held
    tile_rows = contact.shape[0]
    pairs = contact.shape[1] // 128
    span = tile_rows + 2 * HALO
    all_pairs = pairs + 2 * SIDE
    square = 2 * pairs
    fold = tile_rows // square
    half_rows, half_pairs = square // 2, pairs // 2
    begin, end = SIDE, SIDE + pairs
    inner = slice(HALO, HALO + tile_rows)
    r = lax.axis_index("row")
    c = lax.axis_index("col")
    up_edge, down_edge = r == 0, r == rows_of - 1
    left_edge, right_edge = c == 0, c == cols_of - 1

    def there(dr, dc):
        return (r + dr >= 0) & (r + dr < rows_of) & (c + dc >= 0) & (c + dc < cols_of)

    mirror_row = lax.div(c, fold)
    peers = [(mirror_row, fold * r + m) for m in range(fold)]
    slot = lax.rem(c, fold)

    def is_me(peer):
        return (peer[0] == r) & (peer[1] == c)

    loads = [
        pltpu.make_async_copy(
            contact.at[:, pl.ds(128 * j, 128)],
            v1.at[begin + j, pl.ds(HALO, tile_rows), :],
            load_sem.at[j],
        )
        for j in range(pairs)
    ]
    weight_loads = [
        pltpu.make_async_copy(src, dst, weight_sem.at[at])
        for at, (src, dst) in enumerate(zip(weights, held))
    ]
    for load in loads + weight_loads:
        load.start()

    barrier = pltpu.get_barrier_semaphore()
    greeted = jnp.int32(0)
    for dr, dc in SIDES + ENDS:
        ok = there(dr, dc)
        greeted += ok.astype(jnp.int32)

        @pl.when(ok)
        def _():
            pl.semaphore_signal(barrier, inc=1, device_id=(r + dr, c + dc), device_id_type=MESH)

    for peer in peers:
        other = jnp.logical_not(is_me(peer))
        greeted += other.astype(jnp.int32)

        @pl.when(other)
        def _():
            pl.semaphore_signal(barrier, inc=1, device_id=peer, device_id_type=MESH)

    mine, parity = lax.div(r, 2), lax.rem(r, 2)
    home = lax.div(mirror_row, 2) == mine
    away = jnp.logical_not(home)
    relay = (2 * lax.div(mirror_row, 2) + parity, c)

    @pl.when(away)
    def _():
        pl.semaphore_signal(barrier, inc=1, device_id=relay, device_id_type=MESH)
        for m in range(fold):
            giver = (2 * mine + lax.rem(mirror_row, 2), fold * r + m)
            pl.semaphore_signal(barrier, inc=1, device_id=giver, device_id_type=MESH)

    for i in range(rows_of // 2):

        @pl.when(home & (mine != i))
        def _():
            served = 2 * i + parity
            for partner in [(served, c)] + [(mirror_row, fold * served + m) for m in range(fold)]:
                pl.semaphore_signal(barrier, inc=1, device_id=partner, device_id_type=MESH)

    greeted += jnp.where(home, (rows_of // 2 - 1) * (1 + fold), 1 + fold)

    def clear(buf, low, high, lanes=slice(0, 128)):
        width = lanes.stop - lanes.start
        buf[low:high, :, lanes] = jnp.zeros((high - low, span, width), buf.dtype)

    def clear_rows(buf):
        strip = jnp.zeros((all_pairs, HALO, 128), buf.dtype)

        @pl.when(up_edge)
        def _():
            buf[:, 0:HALO, :] = strip

        @pl.when(down_edge)
        def _():
            buf[:, HALO + tile_rows : span, :] = strip

    def clear_outside(buf):
        clear_rows(buf)

        @pl.when(left_edge)
        def _():
            clear(buf, 0, begin)

        @pl.when(right_edge)
        def _():
            clear(buf, end, all_pairs)

    def clear_hidden(hid, s):
        clear_rows(hid)

        @pl.when(left_edge)
        def _():
            clear(hid, 0, begin, slice(0, 64))
            clear(hid, 0, begin - s, slice(64, 128))

        @pl.when(right_edge)
        def _():
            clear(hid, end, all_pairs, slice(0, 64))
            clear(hid, end - s, all_pairs, slice(64, 128))

    class Halo:
        def __init__(self, buf, send, recv):
            self.copies = {}
            for at, (dr, dc) in enumerate(SIDES + ENDS + CORNERS):
                row, rows, to_row = {
                    -1: (HALO, HALO, HALO + tile_rows), 0: (HALO, tile_rows, HALO), 1: (tile_rows, HALO, 0)
                }[dr]
                if dr == 0:
                    col, cols, to_col = {-1: (begin, SIDE, end), 1: (pairs, SIDE, 0)}[dc]
                else:
                    col, cols = {-1: (0, SIDE), 0: (begin, pairs), 1: (end, SIDE)}[dc]
                    to_col = col
                to_device = (jnp.clip(r + dr, 0, rows_of - 1), c)
                if dr == 0:
                    to_device = (r, jnp.clip(c + dc, 0, cols_of - 1))
                self.copies[dr, dc] = pltpu.make_async_remote_copy(
                    src_ref=buf.at[pl.ds(col, cols), pl.ds(row, rows), :],
                    dst_ref=buf.at[pl.ds(to_col, cols), pl.ds(to_row, rows), :],
                    send_sem=send.at[at],
                    recv_sem=recv.at[at],
                    device_id=to_device,
                    device_id_type=MESH,
                )

        def start(self, dr, dc):
            pl.when(there(dr, dc))(self.copies[dr, dc].start)

        def wait_sent(self, dr, dc):
            pl.when(there(dr, dc))(self.copies[dr, dc].wait_send)

        def wait_side(self, dc):
            pl.when(there(0, -dc))(self.copies[0, dc].wait_recv)

        def wait_end(self, dr):
            pl.when(there(-dr, 0))(self.copies[dr, 0].wait_recv)

        def wait_corner(self, dr, dc):
            pl.when(there(-dr, dc))(self.copies[dr, dc].wait_recv)

    def down(buf, hid, at, d, s, s_up, chunks):
        low, n, stride, count = chunks

        def step(i, carry):
            j = low + i * stride
            x = jnp.concatenate(
                [buf[pl.ds(j - s, n)], buf[pl.ds(j, n)], buf[pl.ds(j + s, n)]], axis=-1
            ).reshape(n * span, 384)
            sums = jnp.dot(x, wd[at], preferred_element_type=jnp.float32)
            outer, central = sums[:, :128], sums[:, 128:]
            h = pltpu.roll(outer, d, 0) + central
            h = h + pltpu.roll(pltpu.roll(outer, 64, 1), n * span - d, 0)
            h = jnp.maximum(h + bias[at : at + 1, :], 0.0)
            moved = pltpu.roll(h, 64, 1)
            hid[pl.ds(j, n), :, 0:64] = h.astype(jnp.bfloat16).reshape(n, span, 128)[:, :, 0:64]
            hid[pl.ds(j - s_up, n), :, 64:128] = moved.astype(jnp.bfloat16).reshape(n, span, 128)[
                :, :, 64:128
            ]
            return carry

        lax.fori_loop(0, count, step, 0)
        clear_hidden(hid, s_up)

    def up(hid, at, d, s, chunks, store):
        low, n, stride, count = chunks

        def step(i, carry):
            j = low + i * stride
            x = jnp.concatenate([hid[pl.ds(j - s, n)], hid[pl.ds(j + s, n)]], axis=-1)
            sums = jnp.dot(x.reshape(n * span, 256), wu[at], preferred_element_type=jnp.float32)
            u = pltpu.roll(sums[:, :128], d, 0) + sums[:, 128:256]
            u = u + pltpu.roll(sums[:, 256:], n * span - d, 0)
            u = (u + bias[4 + at : 5 + at, :]).reshape(n, span, 128)
            store(j, n, u)
            return carry

        lax.fori_loop(0, count, step, 0)

    def section(buf, halo, at, store_last):
        (d1, d2), (d3, d4) = BLOCKS
        s1, s2, s3, s4 = max(d1 // 2, 1), d2 // 2, d3 // 2, d4 // 2

        def store(j, n, u):
            v = buf[pl.ds(j, n)].astype(jnp.float32) + u
            middle[pl.ds(j, n)] = v.astype(jnp.bfloat16)

        def one(chunks):
            down(buf, hid1, at, d1, s1, s2, chunks)

        def two(chunks):
            up(hid1, at, d2, s2, chunks, store)
            clear_outside(middle)

        def three(chunks):
            down(middle, hid2, at + 1, d3, s3, s4, chunks)

        def centre(t):
            n = chunk_of(pairs - 2 * t, 8)
            return begin + t, n, n, (pairs - 2 * t) // n

        def sides(t):
            return t, SIDE, end - 2 * t, 2

        t1, t2, t3 = s1, s1 + s2, s1 + s2 + s3
        for dr in (-1, 1):
            halo.wait_end(dr)
        one(centre(t1))
        for dc in (-1, 1):
            halo.wait_side(-dc)
            for dr in (-1, 1):
                halo.start(dr, dc)
        two(centre(t2))
        three(centre(t3))
        for dr, dc in CORNERS:
            halo.wait_corner(dr, dc)
        one(sides(t1))
        two(sides(t2))
        three(sides(t3))
        up(hid2, at + 1, d4, s4, centre(0), store_last)
        for way in SIDES + ENDS + CORNERS:
            halo.wait_sent(*way)

    for load in loads:
        load.wait()
    pl.semaphore_wait(barrier, greeted)
    halo1 = Halo(v1, send1, recv1)
    halo2 = Halo(v2, send2, recv2)
    for way in SIDES + ENDS:
        halo1.start(*way)

    clear_outside(v1)
    clear_outside(v2)
    for ref in (hid1, hid2, wu, bias):
        ref[...] = jnp.zeros(ref.shape, ref.dtype)
    for load in weight_loads:
        load.wait()
    for sec, (dw, db, uw, ub) in enumerate(((fd, fdb, fu, fub), (sd, sdb, su, sub))):
        for block, (d1, d2) in enumerate(BLOCKS):
            at = 2 * sec + block
            wide_down[...] = jnp.zeros(wide_down.shape, wide_down.dtype)
            bias[at : at + 1, 0:32] = db[block : block + 1, :]
            bias[at : at + 1, 32:64] = db[block : block + 1, :]
            bias[4 + at : 5 + at, 0:64] = ub[block : block + 1, :]
            bias[4 + at : 5 + at, 64:128] = ub[block : block + 1, :]
            for p in range(3):
                group = (0, 128, 64)[p]
                for q in range(3):
                    for par in range(2):
                        shift = par + (q - 1) * d1
                        third = 1 + (shift // 2 > 0) - (shift // 2 < 0)
                        lane = third * 128 + (shift % 2) * 64
                        row = group + par * 32
                        wide_down[row : row + 32, lane : lane + 64] = dw[block, p, q]
                        row = q * 64 + par * 32
                        lane = p * 128 + par * 64
                        wu[at, row : row + 32, lane : lane + 64] = uw[block, p, q]
            wd[at] = wide_down[...].T

    def store_first(j, n, u):
        v = middle[pl.ds(j, n), inner, :].astype(jnp.float32) + u[:, inner, :]
        first[pl.ds(j - begin, n)] = v.astype(jnp.bfloat16)

    section(v1, halo1, 0, store_first)

    def piece(half, m):
        return first.at[:, pl.ds(m * square + half * half_rows, half_rows), :]

    for m in range(fold):

        @pl.when(away)
        def _():
            pltpu.make_async_remote_copy(
                src_ref=piece(1, m),
                dst_ref=passing.at[mine, m],
                send_sem=send_m.at[m, 1],
                recv_sem=pass_recv.at[mine, m],
                device_id=relay,
                device_id_type=MESH,
            ).start()

    mirrors = {}
    for half in range(2):
        for m, peer in enumerate(peers):
            remote = pltpu.make_async_remote_copy(
                src_ref=piece(half, m),
                dst_ref=mirror.at[slot, half],
                send_sem=send_m.at[m, half],
                recv_sem=recv_m.at[slot, half],
                device_id=peer,
                device_id_type=MESH,
            )
            here = pltpu.make_async_copy(piece(half, m), mirror.at[slot, half], local_sem.at[half])
            direct = jnp.logical_not(is_me(peer))
            if half == 1:
                direct = direct & home
            pl.when(direct)(remote.start)
            pl.when(is_me(peer))(here.start)
            mirrors[half, m] = (peer, remote, here)

    def passed(i, m):
        return pltpu.make_async_remote_copy(
            src_ref=passing.at[i, m],
            dst_ref=mirror.at[slot, 1],
            send_sem=pass_send.at[i, m],
            recv_sem=recv_m.at[slot, 1],
            device_id=(mirror_row, fold * (2 * i + parity) + m),
            device_id_type=MESH,
        )

    for i in range(rows_of // 2):

        @pl.when(home & (mine != i))
        def _():
            for m in range(fold):
                pltpu.make_async_remote_copy(
                    src_ref=passing.at[i, m],
                    dst_ref=passing.at[i, m],
                    send_sem=pass_send.at[i, m],
                    recv_sem=pass_recv.at[i, m],
                    device_id=(2 * i + parity, c),
                    device_id_type=MESH,
                ).wait_recv()
                passed(i, m).start()

    low_half = lax.broadcasted_iota(jnp.int32, (pairs, 128), 1) < 64
    for half in range(2):
        for m in range(fold):
            peer, remote, here = mirrors[half, m]
            arrived = pltpu.make_async_remote_copy(
                src_ref=mirror.at[m, half],
                dst_ref=mirror.at[m, half],
                send_sem=send_m.at[m, half],
                recv_sem=recv_m.at[m, half],
                device_id=peer,
                device_id_type=MESH,
            )
            pl.when(jnp.logical_not(is_me(peer)))(arrived.wait_recv)
            pl.when(is_me(peer))(here.wait)
        for m in range(fold):
            at = half * fold + m
            wide[at] = mirror[m, half].astype(jnp.float32).reshape(pairs * half_rows, 128)
            for j in range(half_pairs):
                even = wide[at, pl.ds(2 * j, pairs, stride=half_rows), :]
                odd = wide[at, pl.ds(2 * j + 1, pairs, stride=half_rows), :]
                base = (half * half_pairs + j) * tile_rows + m * square
                flipped[pl.ds(base, pairs, stride=2), :] = jnp.where(
                    low_half, even, pltpu.roll(odd, 64, 1)
                )
                flipped[pl.ds(base + 1, pairs, stride=2), :] = jnp.where(
                    low_half, pltpu.roll(even, 64, 1), odd
                )
        low = half * half_pairs
        own = first[low : low + half_pairs].astype(jnp.float32)
        turned = flipped[low * tile_rows : (low + half_pairs) * tile_rows, :]
        both = (own + turned.reshape(half_pairs, tile_rows, 128)) * 0.5
        v2[begin + low : begin + low + half_pairs, inner, :] = both.astype(jnp.bfloat16)
        if pairs >= 2 * SIDE or half == 1:
            halo2.start(0, 2 * half - 1)
    if pairs < 2 * SIDE:
        halo2.start(0, -1)
    for way in ENDS:
        halo2.start(*way)
    for half in range(2):
        for m in range(fold):
            peer, remote, here = mirrors[half, m]
            pl.when(jnp.logical_not(is_me(peer)))(remote.wait_send)
    for i in range(rows_of // 2):

        @pl.when(home & (mine != i))
        def _():
            for m in range(fold):
                passed(i, m).wait_send()

    def store_second(j, n, u):
        v = (middle[pl.ds(j, n), inner, :].astype(jnp.float32) + u[:, inner, :]).astype(jnp.bfloat16)
        for k in range(n):
            out[:, pl.ds(pl.multiple_of((j - begin + k) * 128, 128), 128)] = v[k]

    section(v2, halo2, 2, store_second)


def per_device(rows_of, cols_of, contact, *weights):
    tile_rows = contact.shape[0]
    pairs = contact.shape[1] // 128
    span, all_pairs, square = tile_rows + 2 * HALO, pairs + 2 * SIDE, 2 * pairs
    fold = tile_rows // square
    weights = [w.swapaxes(3, 4) if at in (2, 6) else w for at, w in enumerate(weights)]
    ways = len(SIDES + ENDS + CORNERS)
    buf = pltpu.VMEM((all_pairs, span, 128), jnp.bfloat16)
    return pl.pallas_call(
        functools.partial(kernel, rows_of, cols_of),
        out_shape=jax.ShapeDtypeStruct(contact.shape, jnp.bfloat16),
        in_specs=[pl.BlockSpec(memory_space=pl.ANY)] * (1 + len(weights)),
        out_specs=pl.BlockSpec(memory_space=pltpu.VMEM),
        scratch_shapes=[
            *(pltpu.VMEM(w.shape, w.dtype) for w in weights),
            buf,
            buf,
            buf,
            buf,
            buf,
            pltpu.VMEM((pairs, tile_rows, 128), jnp.bfloat16),
            pltpu.VMEM((fold, 2, pairs, pairs, 128), jnp.bfloat16),
            pltpu.VMEM((rows_of // 2, fold, pairs, pairs, 128), jnp.bfloat16),
            pltpu.VMEM((2 * fold, pairs * pairs, 128), jnp.float32),
            pltpu.VMEM((pairs * tile_rows, 128), jnp.float32),
            pltpu.VMEM((256, 384), jnp.bfloat16),
            pltpu.VMEM((4, 384, 256), jnp.bfloat16),
            pltpu.VMEM((4, 256, 384), jnp.bfloat16),
            pltpu.VMEM((8, 128), jnp.float32),
            pltpu.SemaphoreType.DMA((ways,)),
            pltpu.SemaphoreType.DMA((ways,)),
            pltpu.SemaphoreType.DMA((ways,)),
            pltpu.SemaphoreType.DMA((ways,)),
            pltpu.SemaphoreType.DMA((fold, 2)),
            pltpu.SemaphoreType.DMA((fold, 2)),
            pltpu.SemaphoreType.DMA((rows_of // 2, fold)),
            pltpu.SemaphoreType.DMA((rows_of // 2, fold)),
            pltpu.SemaphoreType.DMA((2,)),
            pltpu.SemaphoreType.DMA((pairs,)),
            pltpu.SemaphoreType.DMA((len(weights),)),
        ],
        compiler_params=pltpu.CompilerParams(
            collective_id=0, has_side_effects=True, vmem_limit_bytes=56 * 1024 * 1024
        ),
    )(contact, *weights)


def solution(mesh):
    in_specs = (P("row", "col"), P(), P(), P(), P(), P(), P(), P(), P())
    return jax.shard_map(
        functools.partial(per_device, mesh.shape["row"], mesh.shape["col"]),
        mesh=mesh,
        in_specs=in_specs,
        out_specs=P("row", "col"),
        check_vma=False,
    )
```

profile of v0, /device:TPU:13, one launch (start us, length us, event | category | flops | bytes accessed | tf_op | source)
XLA Modules:
  0.0 41.7 jit_solution(16946715629491994082)
XLA Ops:
  0.0 40.0 %shard_map.91 = bf16[64,2048]{1,0:T(8,128)(2,1)} custom-call(bf16[64,2048]{1,0:T(8,128)(2,1)} %contact.1, bf16[2,3,3,32,64]{4,3,2,1,0:T(8,128)(2,1)} %refs_0_.1, f32[2,32]{1,0:T(2,128)} %refs_1_.1, bf16[2,3,3,32,64]{4,3,2,1,0:T(8,128)(2,1)} %bitcast.2, f32[2,64]{1,0:T(2,128)} %refs_3_.1, bf16[2,3,3,32,64]{4,3,2,1,0:T(8,128)(2,1)} %refs_4_.1, ...), custom_call_target="tpu_custom_call" | custom-call | tf_op jit(solution)/shard_map/pallas_call | solution.py:439
  40.0 1.7 %copy.11 = bf16[64,2048]{1,0:T(8,128)(2,1)} copy(bf16[64,2048]{1,0:T(8,128)(2,1)} %shard_map.91) | data formatting | bytes 524288
where the time goes:
time: 41.9 us; the launch traced here: 41.7 us
  Pallas kernels  40 us (95%)
  local copies, waits for them, and re-layouts  1.67 us (4%)
    pallas_call x1, Pallas kernels, per_device(): pl.pallas_call(functools.partial(kernel, rows_of, cols_of), out_shape=jax...  40 us
    unnamed x1, local copies, waits for them, and re-layouts  1.67 us

commit v1 on v0

--- a/solution.py
+++ b/solution.py
@@ -12,6 +12,7 @@
 SIDE = HALO // 2
 BLOCKS = ((1, 2), (4, 8))
 SIDES = ((0, -1), (0, 1))
+PARTS = (-1, 1, 0)
 ENDS = ((-1, 0), (1, 0))
 CORNERS = ((-1, -1), (-1, 1), (1, -1), (1, 1))
 
@@ -151,26 +152,33 @@
     class Halo:
         def __init__(self, buf, send, recv):
             self.copies = {}
-            for at, (dr, dc) in enumerate(SIDES + ENDS + CORNERS):
-                row, rows, to_row = {
-                    -1: (HALO, HALO, HALO + tile_rows), 0: (HALO, tile_rows, HALO), 1: (tile_rows, HALO, 0)
-                }[dr]
-                if dr == 0:
-                    col, cols, to_col = {-1: (begin, SIDE, end), 1: (pairs, SIDE, 0)}[dc]
-                else:
-                    col, cols = {-1: (0, SIDE), 0: (begin, pairs), 1: (end, SIDE)}[dc]
-                    to_col = col
-                to_device = (jnp.clip(r + dr, 0, rows_of - 1), c)
-                if dr == 0:
-                    to_device = (r, jnp.clip(c + dc, 0, cols_of - 1))
+            for at, (dr, dc) in enumerate(ENDS + CORNERS):
+                row, to_row = (HALO, HALO + tile_rows) if dr < 0 else (tile_rows, 0)
+                col, cols = {-1: (0, SIDE), 0: (begin, pairs), 1: (end, SIDE)}[dc]
                 self.copies[dr, dc] = pltpu.make_async_remote_copy(
-                    src_ref=buf.at[pl.ds(col, cols), pl.ds(row, rows), :],
-                    dst_ref=buf.at[pl.ds(to_col, cols), pl.ds(to_row, rows), :],
+                    src_ref=buf.at[pl.ds(col, cols), pl.ds(row, HALO), :],
+                    dst_ref=buf.at[pl.ds(col, cols), pl.ds(to_row, HALO), :],
                     send_sem=send.at[at],
                     recv_sem=recv.at[at],
-                    device_id=to_device,
+                    device_id=(jnp.clip(r + dr, 0, rows_of - 1), c),
                     device_id_type=MESH,
                 )
+            at = len(ENDS + CORNERS)
+            for _, dc in SIDES:
+                col, to_col = (begin, end) if dc < 0 else (pairs, 0)
+                for part in PARTS:
+                    row, rows = {
+                        -1: (HALO, HALO), 0: (2 * HALO, tile_rows - 2 * HALO), 1: (tile_rows, HALO)
+                    }[part]
+                    self.copies[0, dc, part] = pltpu.make_async_remote_copy(
+                        src_ref=buf.at[pl.ds(col, SIDE), pl.ds(row, rows), :],
+                        dst_ref=buf.at[pl.ds(to_col, SIDE), pl.ds(row, rows), :],
+                        send_sem=send.at[at],
+                        recv_sem=recv.at[at],
+                        device_id=(r, jnp.clip(c + dc, 0, cols_of - 1)),
+                        device_id_type=MESH,
+                    )
+                    at += 1
 
         def start(self, dr, dc):
             pl.when(there(dr, dc))(self.copies[dr, dc].start)
@@ -178,8 +186,14 @@
         def wait_sent(self, dr, dc):
             pl.when(there(dr, dc))(self.copies[dr, dc].wait_send)
 
-        def wait_side(self, dc):
-            pl.when(there(0, -dc))(self.copies[0, dc].wait_recv)
+        def start_side(self, dc, part):
+            pl.when(there(0, dc))(self.copies[0, dc, part].start)
+
+        def wait_side_sent(self, dc, part):
+            pl.when(there(0, dc))(self.copies[0, dc, part].wait_send)
+
+        def wait_side(self, dc, part):
+            pl.when(there(0, -dc))(self.copies[0, dc, part].wait_recv)
 
         def wait_end(self, dr):
             pl.when(there(-dr, 0))(self.copies[dr, 0].wait_recv)
@@ -255,27 +269,35 @@
             halo.wait_end(dr)
         one(centre(t1))
         for dc in (-1, 1):
-            halo.wait_side(-dc)
             for dr in (-1, 1):
+                halo.wait_side(-dc, dr)
                 halo.start(dr, dc)
         two(centre(t2))
         three(centre(t3))
+        for dc in (-1, 1):
+            halo.wait_side(dc, 0)
         for dr, dc in CORNERS:
             halo.wait_corner(dr, dc)
         one(sides(t1))
         two(sides(t2))
         three(sides(t3))
         up(hid2, at + 1, d4, s4, centre(0), store_last)
-        for way in SIDES + ENDS + CORNERS:
+        for way in ENDS + CORNERS:
             halo.wait_sent(*way)
+        for _, dc in SIDES:
+            for part in PARTS:
+                halo.wait_side_sent(dc, part)
 
     for load in loads:
         load.wait()
     pl.semaphore_wait(barrier, greeted)
     halo1 = Halo(v1, send1, recv1)
     halo2 = Halo(v2, send2, recv2)
-    for way in SIDES + ENDS:
+    for way in ENDS:
         halo1.start(*way)
+    for part in PARTS:
+        for _, dc in SIDES:
+            halo1.start_side(dc, part)
 
     clear_outside(v1)
     clear_outside(v2)
@@ -403,10 +425,8 @@
         turned = flipped[low * tile_rows : (low + half_pairs) * tile_rows, :]
         both = (own + turned.reshape(half_pairs, tile_rows, 128)) * 0.5
         v2[begin + low : begin + low + half_pairs, inner, :] = both.astype(jnp.bfloat16)
-        if pairs >= 2 * SIDE or half == 1:
-            halo2.start(0, 2 * half - 1)
-    if pairs < 2 * SIDE:
-        halo2.start(0, -1)
+        for part in PARTS:
+            halo2.start_side(2 * half - 1, part)
     for way in ENDS:
         halo2.start(*way)
     for half in range(2):
@@ -434,7 +454,7 @@
     span, all_pairs, square = tile_rows + 2 * HALO, pairs + 2 * SIDE, 2 * pairs
     fold = tile_rows // square
     weights = [w.swapaxes(3, 4) if at in (2, 6) else w for at, w in enumerate(weights)]
-    ways = len(SIDES + ENDS + CORNERS)
+    ways = len(SIDES) * len(PARTS) + len(ENDS + CORNERS)
     buf = pltpu.VMEM((all_pairs, span, 128), jnp.bfloat16)
     return pl.pallas_call(
         functools.partial(kernel, rows_of, cols_of),

time: 41.9 us -> 40.1 us (0.957)
  the two profiles are of different devices: /device:TPU:13 before, /device:TPU:9 now
where the time goes in v1:
time: 40.1 us; the launch traced here: 39.9 us
  Pallas kernels  38.2 us (95%)
  local copies, waits for them, and re-layouts  1.67 us (4%)
    pallas_call x1, Pallas kernels, per_device(): pl.pallas_call(functools.partial(kernel, rows_of, cols_of), out_shape=jax...  38.2 us
    unnamed x1, local copies, waits for them, and re-layouts  1.67 us

profile of v1, /device:TPU:9, one launch (start us, length us, event | category | flops | bytes accessed | tf_op | source)
XLA Modules:
  0.0 39.9 jit_solution(6494297797657549444)
XLA Ops:
  0.0 38.2 %shard_map.91 = bf16[64,2048]{1,0:T(8,128)(2,1)} custom-call(bf16[64,2048]{1,0:T(8,128)(2,1)} %contact.1, bf16[2,3,3,32,64]{4,3,2,1,0:T(8,128)(2,1)} %refs_0_.1, f32[2,32]{1,0:T(2,128)} %refs_1_.1, bf16[2,3,3,32,64]{4,3,2,1,0:T(8,128)(2,1)} %bitcast.2, f32[2,64]{1,0:T(2,128)} %refs_3_.1, bf16[2,3,3,32,64]{4,3,2,1,0:T(8,128)(2,1)} %refs_4_.1, ...), custom_call_target="tpu_custom_call" | custom-call | tf_op jit(solution)/shard_map/pallas_call | solution.py:459
  38.2 1.7 %copy.11 = bf16[64,2048]{1,0:T(8,128)(2,1)} copy(bf16[64,2048]{1,0:T(8,128)(2,1)} %shard_map.91) | data formatting | bytes 524288

commit v2 on v1

--- a/solution.py
+++ b/solution.py
@@ -55,6 +55,46 @@
     def is_me(peer):
         return (peer[0] == r) & (peer[1] == c)
 
+    barrier = pltpu.get_barrier_semaphore()
+    greeted = jnp.int32(0)
+    for dr, dc in SIDES + ENDS:
+        ok = there(dr, dc)
+        greeted += ok.astype(jnp.int32)
+
+        @pl.when(ok)
+        def _():
+            pl.semaphore_signal(barrier, inc=1, device_id=(r + dr, c + dc), device_id_type=MESH)
+
+    for peer in peers:
+        other = jnp.logical_not(is_me(peer))
+        greeted += other.astype(jnp.int32)
+
+        @pl.when(other)
+        def _():
+            pl.semaphore_signal(barrier, inc=1, device_id=peer, device_id_type=MESH)
+
+    mine, parity = lax.div(r, 2), lax.rem(r, 2)
+    home = lax.div(mirror_row, 2) == mine
+    away = jnp.logical_not(home)
+    relay = (2 * lax.div(mirror_row, 2) + parity, c)
+
+    @pl.when(away)
+    def _():
+        pl.semaphore_signal(barrier, inc=1, device_id=relay, device_id_type=MESH)
+        for m in range(fold):
+            giver = (2 * mine + lax.rem(mirror_row, 2), fold * r + m)
+            pl.semaphore_signal(barrier, inc=1, device_id=giver, device_id_type=MESH)
+
+    for i in range(rows_of // 2):
+
+        @pl.when(home & (mine != i))
+        def _():
+            served = 2 * i + parity
+            for partner in [(served, c)] + [(mirror_row, fold * served + m) for m in range(fold)]:
+                pl.semaphore_signal(barrier, inc=1, device_id=partner, device_id_type=MESH)
+
+    greeted += jnp.where(home, (rows_of // 2 - 1) * (1 + fold), 1 + fold)
+
     loads = [
         pltpu.make_async_copy(
             contact.at[:, pl.ds(128 * j, 128)],
@@ -69,46 +109,6 @@
     ]
     for load in loads + weight_loads:
         load.start()
-
-    barrier = pltpu.get_barrier_semaphore()
-    greeted = jnp.int32(0)
-    for dr, dc in SIDES + ENDS:
-        ok = there(dr, dc)
-        greeted += ok.astype(jnp.int32)
-
-        @pl.when(ok)
-        def _():
-            pl.semaphore_signal(barrier, inc=1, device_id=(r + dr, c + dc), device_id_type=MESH)
-
-    for peer in peers:
-        other = jnp.logical_not(is_me(peer))
-        greeted += other.astype(jnp.int32)
-
-        @pl.when(other)
-        def _():
-            pl.semaphore_signal(barrier, inc=1, device_id=peer, device_id_type=MESH)
-
-    mine, parity = lax.div(r, 2), lax.rem(r, 2)
-    home = lax.div(mirror_row, 2) == mine
-    away = jnp.logical_not(home)
-    relay = (2 * lax.div(mirror_row, 2) + parity, c)
-
-    @pl.when(away)
-    def _():
-        pl.semaphore_signal(barrier, inc=1, device_id=relay, device_id_type=MESH)
-        for m in range(fold):
-            giver = (2 * mine + lax.rem(mirror_row, 2), fold * r + m)
-            pl.semaphore_signal(barrier, inc=1, device_id=giver, device_id_type=MESH)
-
-    for i in range(rows_of // 2):
-
-        @pl.when(home & (mine != i))
-        def _():
-            served = 2 * i + parity
-            for partner in [(served, c)] + [(mirror_row, fold * served + m) for m in range(fold)]:
-                pl.semaphore_signal(barrier, inc=1, device_id=partner, device_id_type=MESH)
-
-    greeted += jnp.where(home, (rows_of // 2 - 1) * (1 + fold), 1 + fold)
 
     def clear(buf, low, high, lanes=slice(0, 128)):
         width = lanes.stop - lanes.start
@@ -261,8 +261,8 @@
             n = chunk_of(pairs - 2 * t, 8)
             return begin + t, n, n, (pairs - 2 * t) // n
 
-        def sides(t):
-            return t, SIDE, end - 2 * t, 2
+        def side_chunk(t, i):
+            return t + i * (end - 2 * t), SIDE, 0, 1
 
         t1, t2, t3 = s1, s1 + s2, s1 + s2 + s3
         for dr in (-1, 1):
@@ -274,13 +274,22 @@
                 halo.start(dr, dc)
         two(centre(t2))
         three(centre(t3))
-        for dc in (-1, 1):
-            halo.wait_side(dc, 0)
-        for dr, dc in CORNERS:
-            halo.wait_corner(dr, dc)
-        one(sides(t1))
-        two(sides(t2))
-        three(sides(t3))
+
+        def side(i, carry):
+            for k, (_, dc) in enumerate(SIDES):
+
+                @pl.when(i == k)
+                def _():
+                    halo.wait_side(-dc, 0)
+                    for dr in (-1, 1):
+                        halo.wait_corner(dr, dc)
+
+            one(side_chunk(t1, i))
+            two(side_chunk(t2, i))
+            three(side_chunk(t3, i))
+            return carry
+
+        lax.fori_loop(0, 2, side, 0)
         up(hid2, at + 1, d4, s4, centre(0), store_last)
         for way in ENDS + CORNERS:
             halo.wait_sent(*way)

time: 40.1 us -> 40.9 us (1.020)
  Pallas kernels: 38.2 us -> 39.1 us
    pallas_call x1, Pallas kernels: 38.2 us -> 39.1 us  [per_device(): pl.pallas_call(functools.partial(kernel, rows_of, cols_of), out_shape=jax...]
where the time goes in v2:
time: 40.9 us; the launch traced here: 40.8 us
  Pallas kernels  39.1 us (96%)
  local copies, waits for them, and re-layouts  1.67 us (4%)
    pallas_call x1, Pallas kernels, per_device(): pl.pallas_call(functools.partial(kernel, rows_of, cols_of), out_shape=jax...  39.1 us
    unnamed x1, local copies, waits for them, and re-layouts  1.67 us

profile of v2, /device:TPU:9, one launch (start us, length us, event | category | flops | bytes accessed | tf_op | source)
XLA Modules:
  0.0 40.8 jit_solution(9139202216363850855)
XLA Ops:
  0.0 39.1 %shard_map.91 = bf16[64,2048]{1,0:T(8,128)(2,1)} custom-call(bf16[64,2048]{1,0:T(8,128)(2,1)} %contact.1, bf16[2,3,3,32,64]{4,3,2,1,0:T(8,128)(2,1)} %refs_0_.1, f32[2,32]{1,0:T(2,128)} %refs_1_.1, bf16[2,3,3,32,64]{4,3,2,1,0:T(8,128)(2,1)} %bitcast.2, f32[2,64]{1,0:T(2,128)} %refs_3_.1, bf16[2,3,3,32,64]{4,3,2,1,0:T(8,128)(2,1)} %refs_4_.1, ...), custom_call_target="tpu_custom_call" | custom-call | tf_op jit(solution)/shard_map/pallas_call | solution.py:468
  39.1 1.7 %copy.11 = bf16[64,2048]{1,0:T(8,128)(2,1)} copy(bf16[64,2048]{1,0:T(8,128)(2,1)} %shard_map.91) | data formatting | bytes 524288
